TPU v7x, 128 devices: a whole 4x4x4 slice. The times are simulated.
128 devices in a mesh: wide: 16 (over z, x), narrow: 8 (over y, core).
Axes of the slice: x: 4, y: 4, z: 4, core: 2. Of those that a mesh axis runs over, the one named last changes fastest.
Arguments:
- samples: bfloat16 [16, 4096, 48, 128], P('wide', 'narrow'), may hold values from -6 to 6
- spacing: bfloat16 [16, 4096, 48], P('wide', 'narrow'), may hold values from 0.00019931793 to 0.0049743652
- region_ids: int32 [16, 4096, 1], P('wide', 'narrow'), may hold values from 0 to 511; in each aligned block of 512 rows (0 to 511, 512 to 1023, ..., all dimensions but the last counted through in order) at most 2 rows name the same one
- directions: int32 [4096], P('narrow'), may hold values 0 or 1
- w_in: bfloat16 [512, 128, 256], P(('wide', 'narrow')), may hold values from -0.75 to 0.75
- w_mid: bfloat16 [512, 2, 256, 256], P(('wide', 'narrow')), may hold values from -0.5 to 0.5
- w_out: bfloat16 [512, 4, 256], P(('wide', 'narrow')), may hold values from -0.75 to 0.75
Outputs:
- ray_colour: float32 [3, 4096], P(None, 'narrow')
Inputs may be any that keep to these rules, and one draw needn't show every extreme that they name: `region_ids`: among the 512 segments of one device (aligned blocks of rows of the flattened first two dimensions) at most 2 name any one region, a bound that some block reaches there.
All inputs are finite; a program needn't handle non-finite values. No bound on the sum of `directions` on one device may be relied on, other than what follows from the above.
Results may differ from a plain program's by a relative error of at most 0.00058.
Values may be sent and summed in bfloat16 or wider, within the bound.
A program may use at most 128 MiB of HBM per device.

v0:
```python
import jax
import jax.numpy as jnp
from jax import lax
from jax.sharding import PartitionSpec as P


def prefix_2(array, axis, combine, identity, reverse):
    count, position = (lax.axis_size(axis), lax.axis_index(axis))
    everything = lax.all_gather(array, axis)
    start = jnp.broadcast_to(jnp.asarray(identity, array.dtype), array.shape)

    def hop(k, before):
        at = count - 1 - k if reverse else k
        reached = at > position if reverse else at < position
        new = combine(before, everything[at])
        return jnp.where(reached, new, before)

    return lax.fori_loop(0, count, hop, start)


def composite(raw_out, spacing_part):
    density = jax.nn.softplus(raw_out[0])
    colours = jax.nn.sigmoid(raw_out[1:4])
    optical = density * spacing_part.astype(jnp.float32)
    before_sum = jnp.cumsum(optical, axis=-1) - optical
    sample_weight = jnp.exp(-before_sum) * -jnp.expm1(-optical)
    seg_colour = jnp.sum(sample_weight * colours, axis=-1)
    seg_depth = jnp.sum(optical, axis=-1)
    return jnp.stack([seg_colour[0], seg_colour[1], seg_colour[2], seg_depth], axis=-1)


def accumulate(earlier, later):
    return earlier + later


def on_device(samples, spacing, region_ids, directions, w_in, w_mid, w_out):
    wide_size = lax.axis_size("wide")
    narrow_size = lax.axis_size("narrow")
    devices_all = wide_size * narrow_size
    reg_local = w_in.shape[0]
    ray_local = samples.shape[1]
    sample_len = samples.shape[2]
    width_in = samples.shape[3]
    region_all = reg_local * devices_all
    capacity = max(2, 2 * ray_local // region_all)
    slot_total = region_all * capacity
    region_row = region_ids.reshape(ray_local)
    matches = region_row[:, None] == region_row[None, :]
    positions = jnp.arange(ray_local, dtype=jnp.int32)
    earlier = positions[None, :] < positions[:, None]
    arrival = jnp.sum(jnp.logical_and(matches, earlier), axis=1)
    slot_index = region_row * capacity + arrival
    source_row = jnp.full((slot_total,), ray_local, jnp.int32).at[slot_index].set(positions)
    ray_rows = jnp.concatenate(
        [
            samples.reshape(ray_local, sample_len, width_in),
            jnp.zeros((1, sample_len, width_in), samples.dtype),
        ],
        axis=0,
    )
    gap_rows = jnp.concatenate(
        [spacing.reshape(ray_local, sample_len), jnp.zeros((1, sample_len), spacing.dtype)], axis=0
    )
    send_features = jnp.take(ray_rows, source_row, axis=0)
    send_spacing = jnp.take(gap_rows, source_row, axis=0)
    features = lax.all_to_all(
        send_features.reshape(devices_all, reg_local, capacity, sample_len, width_in),
        ("wide", "narrow"),
        split_axis=0,
        concat_axis=0,
        tiled=True,
    )
    spacing_part = lax.all_to_all(
        send_spacing.reshape(devices_all, reg_local, capacity, sample_len),
        ("wide", "narrow"),
        split_axis=0,
        concat_axis=0,
        tiled=True,
    )
    results = []
    for region in range(reg_local):
        inputs = features[:, region].reshape(-1, width_in)
        hidden = jax.nn.relu(
            jnp.dot(inputs, w_in[region], preferred_element_type=jnp.float32)
        ).astype(jnp.bfloat16)
        for layer_index in range(w_mid.shape[1]):
            hidden = jax.nn.relu(
                jnp.dot(hidden, w_mid[region, layer_index], preferred_element_type=jnp.float32)
            ).astype(jnp.bfloat16)
        raw_out = jnp.einsum("nh,ch->cn", hidden, w_out[region], preferred_element_type=jnp.float32)
        part_gap = spacing_part[:, region]
        raw_out = raw_out.reshape((4,) + part_gap.shape)
        results.append(composite(raw_out, part_gap))
    partial_here = jnp.stack(results, axis=1)
    returned = lax.all_to_all(
        partial_here, ("wide", "narrow"), split_axis=0, concat_axis=0, tiled=True
    )
    mine = jnp.take(returned.reshape(slot_total, 4), slot_index, axis=0)
    seg_depth = mine[:, 3]
    zero_depth = jnp.zeros_like(seg_depth)
    ahead = prefix_2(seg_depth, "wide", accumulate, zero_depth, False)
    behind = prefix_2(seg_depth, "wide", accumulate, zero_depth, True)
    prefix = jnp.where(directions == 1, behind, ahead)
    light = jnp.exp(-prefix)
    light_term = (light[:, None] * mine[:, :3]).T
    return lax.psum(light_term, "wide")


def solution(mesh):
    in_specs = (
        P("wide", "narrow", None, None),
        P("wide", "narrow", None),
        P("wide", "narrow", None),
        P("narrow"),
        P(("wide", "narrow"), None, None),
        P(("wide", "narrow"), None, None, None),
        P(("wide", "narrow"), None, None),
    )
    out_specs = P(None, "narrow")
    return jax.shard_map(
        on_device, mesh=mesh, in_specs=in_specs, out_specs=out_specs, check_vma=False
    )
```

profile of v0, /device:TPU:0, one launch (start us, length us, event | category | flops | bytes accessed | tf_op | source)
XLA Modules:
  0.0 437.7 jit_solution(7834109380636797932)
XLA Ops:
  0.0 1.0 convert_reduce_fusion
  1.0 0.7 compare_select_fusion.4
  1.7 2.4 scatter_custom_fusion
  4.2 0.3 broadcast_in_dim.53
  4.4 0.9 copy.228
  5.4 3.2 gather_fusion.1
  8.6 0.8 broadcast_select_fusion.1
  9.5 0.9 reshape.461
  10.5 11.1 %all-to-all-start.1 = ((bf16[128,2,192]{2,1,0:T(2,128)(2,1)}), bf16[128,2,192]{2,1,0:T(2,128)(2,1)S(1)}, u32[]{:S(2)}, u32[]{:S(2)}) async-start(bf16[128,2,192]{2,1,0:T(2,128)(2,1)} %reshape.461), calls=%async_computation.1 | async-start | bytes 262144 | tf_op jit(solution)/shard_map/all_to_all | solution.py:73
  21.6 6.5 %concatenate.6 = bf16[513,48,128]{2,1,0:T(8,128)(2,1)} pad(bf16[512,48,128]{2,1,0:T(8,128)(2,1)} %bitcast.162, bf16[]{:T(256)} %constant.149.clone.1), padding=0_1x0_0x0_0 | pad | bytes 12595202 | tf_op jit(solution)/shard_map/concatenate | solution.py:54
  28.1 14.5 %gather_fusion = bf16[1024,48,128]{2,1,0:T(8,128)(2,1)} fusion(bf16[513,48,128]{2,1,0:T(8,128)(2,1)} %concatenate.6, s32[1024]{0:T(1024)S(1)} %fusion.90), kind=kCustom, calls=%fused_computation | custom fusion | bytes 25169920 | tf_op jit(solution)/shard_map/jit(_take)/gather | solution.py:64
  42.6 10.9 %broadcast_select_fusion = bf16[128,4,2,48,128]{4,3,2,1,0:T(8,128)(2,1)} fusion(bf16[128,4,2,48,128]{4,3,2,1,0:T(8,128)(2,1)} %bitcast.160, pred[128,4,2]{2,1,0:T(4,128)(4,1)S(1)} %broadcast_in_dim.53), kind=kLoop, calls=%fused_computation.36 | loop fusion | flops 6291456 | bytes 25166848 | tf_op jit(solution)/shard_map/jit(_take)/select_n | solution.py:64
  53.5 10.2 %all-to-all-start = ((bf16[128,4,2,48,128]{4,3,2,1,0:T(8,128)(2,1)}), bf16[128,4,2,48,128]{4,3,2,1,0:T(8,128)(2,1)}, u32[]{:S(2)}, u32[]{:S(2)}) async-start(bf16[128,4,2,48,128]{4,3,2,1,0:T(8,128)(2,1)} %broadcast_select_fusion), calls=%async_computation | async-start | bytes 25165824 | tf_op jit(solution)/shard_map/all_to_all | solution.py:66
  63.8 0.2 reshape.462
  64.0 0.4 fusion.118
  64.4 0.7 copy.292
  65.1 0.7 copy.293
  65.8 0.7 copy.294
  66.4 0.7 copy.295
  67.2 148.5 %all-to-all-done = bf16[128,4,2,48,128]{4,3,2,1,0:T(8,128)(2,1)} async-done(((bf16[128,4,2,48,128]{4,3,2,1,0:T(8,128)(2,1)}), bf16[128,4,2,48,128]{4,3,2,1,0:T(8,128)(2,1)}, u32[]{:S(2)}, u32[]{:S(2)}) %all-to-all-start) | async-done | bytes 12582944 | tf_op jit(solution)/shard_map/all_to_all | solution.py:66
  215.6 8.9 %fusion.117 = (bf16[128,1,2,48,128]{4,3,2,1,0:T(8,128)(2,1)}, bf16[128,1,2,48,128]{4,3,2,1,0:T(8,128)(2,1)S(1)}, bf16[128,1,2,48,128]{4,3,2,1,0:T(8,128)(2,1)}, bf16[128,1,2,48,128]{4,3,2,1,0:T(8,128)(2,1)}) fusion(bf16[128,4,2,48,128]{4,3,2,1,0:T(8,128)(2,1)} %all-to-all-done), kind=kLoop, calls=%fused_computation.172 | loop fusion | bytes 25165824 | tf_op jit(solution)/shard_map/slice | solution.py:82
  224.5 8.1 %fusion.4 = bf16[12288,256]{1,0:T(8,128)(2,1)} fusion(bf16[12288,128]{1,0:T(8,128)(2,1)} %bitcast.166, bf16[4,2,256,256]{3,2,1,0:T(8,128)(2,1)} %param.16, bf16[4,128,256]{2,1,0:T(8,128)(2,1)S(1)} %copy-done.11), kind=kOutput, calls=%fused_computation.24 | convolution fusion | flops 2428502016 | bytes 9633792 | tf_op jit(solution)/shard_map/dot_general | solution.py:88
  232.6 6.3 %convolution_bitcast_fusion.3 = f32[4,12288]{1,0:T(4,128)S(1)} fusion(bf16[12288,256]{1,0:T(8,128)(2,1)} %fusion.4, bf16[4,2,256,256]{3,2,1,0:T(8,128)(2,1)} %param.16, bf16[4,4,256]{2,1,0:T(4,128)(2,1)S(1)} %copy-done.12), kind=kOutput, calls=%fused_computation.35 | convolution fusion | flops 1642070016 | bytes 6621184 | tf_op jit(solution)/shard_map/nh,ch->cn/dot_general | solution.py:90
  239.0 0.8 slice_reduce_fusion.3
  239.7 0.8 fusion.25
  240.5 8.1 %fusion.6 = bf16[12288,256]{1,0:T(8,128)(2,1)} fusion(bf16[12288,128]{1,0:T(8,128)(2,1)} %bitcast.165, bf16[4,2,256,256]{3,2,1,0:T(8,128)(2,1)} %param.16, bf16[4,128,256]{2,1,0:T(8,128)(2,1)} %param.15), kind=kOutput, calls=%fused_computation.26 | convolution fusion | flops 2428502016 | bytes 9633792 | tf_op jit(solution)/shard_map/dot_general | solution.py:88
  248.6 6.7 %convolution_bitcast_fusion.2 = f32[4,12288]{1,0:T(4,128)S(1)} fusion(bf16[12288,256]{1,0:T(8,128)(2,1)} %fusion.6, bf16[4,2,256,256]{3,2,1,0:T(8,128)(2,1)} %param.16, bf16[4,4,256]{2,1,0:T(4,128)(2,1)S(1)} %copy-done.12), kind=kOutput, calls=%fused_computation.34 | convolution fusion | flops 1642070016 | bytes 6621184 | tf_op jit(solution)/shard_map/nh,ch->cn/dot_general | solution.py:90
  255.3 0.7 slice_reduce_fusion.2
  256.1 0.1 fusion.22
  256.2 8.1 %fusion.8 = bf16[12288,256]{1,0:T(8,128)(2,1)} fusion(bf16[12288,128]{1,0:T(8,128)(2,1)} %bitcast.164, bf16[4,2,256,256]{3,2,1,0:T(8,128)(2,1)} %param.16, bf16[4,128,256]{2,1,0:T(8,128)(2,1)} %param.15), kind=kOutput, calls=%fused_computation.28 | convolution fusion | flops 2428502016 | bytes 9633792 | tf_op jit(solution)/shard_map/dot_general | solution.py:88
  264.3 6.3 %convolution_bitcast_fusion.1 = f32[4,12288]{1,0:T(4,128)S(1)} fusion(bf16[12288,256]{1,0:T(8,128)(2,1)} %fusion.8, bf16[4,2,256,256]{3,2,1,0:T(8,128)(2,1)} %param.16, bf16[4,4,256]{2,1,0:T(4,128)(2,1)S(1)} %copy-done.12), kind=kOutput, calls=%fused_computation.33 | convolution fusion | flops 1642070016 | bytes 6621184 | tf_op jit(solution)/shard_map/nh,ch->cn/dot_general | solution.py:90
  270.7 0.7 copy-done.1
  271.3 0.7 slice_reduce_fusion.1
  272.1 1.0 fusion.19
  273.1 7.3 %fusion.10 = bf16[12288,256]{1,0:T(8,128)(2,1)} fusion(bf16[12288,128]{1,0:T(8,128)(2,1)S(1)} %bitcast.163, bf16[4,2,256,256]{3,2,1,0:T(8,128)(2,1)} %param.16, bf16[4,128,256]{2,1,0:T(8,128)(2,1)} %param.15), kind=kOutput, calls=%fused_computation.30 | convolution fusion | flops 2428502016 | bytes 9633792 | tf_op jit(solution)/shard_map/dot_general | solution.py:88
  280.5 6.4 %convolution_bitcast_fusion = f32[4,12288]{1,0:T(4,128)S(1)} fusion(bf16[12288,256]{1,0:T(8,128)(2,1)} %fusion.10, bf16[4,2,256,256]{3,2,1,0:T(8,128)(2,1)} %param.16, bf16[4,4,256]{2,1,0:T(4,128)(2,1)S(1)} %copy-done.12), kind=kOutput, calls=%fused_computation.32 | convolution fusion | flops 1642070016 | bytes 6621184 | tf_op jit(solution)/shard_map/nh,ch->cn/dot_general | solution.py:90
  286.8 0.1 slice_reduce_fusion
  287.0 0.1 fusion.16
  287.1 0.2 squeeze.85
  287.4 0.3 squeeze.90
  288.1 0.7 div.25
  288.8 0.5 multiply_reduce_fusion.3
  289.7 0.7 div.27
  290.4 0.5 multiply_reduce_fusion.2
  291.1 0.3 squeeze.95
  291.5 0.3 squeeze.100
  292.1 0.7 div.29
  292.8 0.5 multiply_reduce_fusion.1
  293.8 0.7 div.31
  294.5 0.5 multiply_reduce_fusion
  295.3 1.0 copy.281
  296.3 12.0 %all-to-all-start.2 = ((f32[128,4,2,4]{3,1,2,0:T(4,128)}), f32[128,4,2,4]{3,1,2,0:T(4,128)S(1)}, u32[]{:S(2)}, u32[]{:S(2)}) async-start(f32[128,4,2,4]{3,1,2,0:T(4,128)} %copy.281), calls=%async_computation.2 | async-start | bytes 1048576 | tf_op jit(solution)/shard_map/all_to_all | solution.py:95
  308.3 13.5 %all-to-all-done.2 = f32[128,4,2,4]{3,1,2,0:T(4,128)S(1)} async-done(((f32[128,4,2,4]{3,1,2,0:T(4,128)}), f32[128,4,2,4]{3,1,2,0:T(4,128)S(1)}, u32[]{:S(2)}, u32[]{:S(2)}) %all-to-all-start.2) | async-done | bytes 16416 | tf_op jit(solution)/shard_map/all_to_all | solution.py:95
  321.8 0.3 copy.282
  322.1 1.0 gather_fusion.2
  323.1 0.1 broadcast_select_fusion.2
  323.3 0.1 slice.226
  323.4 33.5 %all-gather = f32[8192,1]{1,0:T(8,128)} all-gather(f32[512,1]{1,0:T(8,128)S(1)} %slice.226), channel_id=2, replica_groups=mesh['wide'=16,'narrow'=8] {'wide'}, dimensions={0}, use_global_device_ids=true | all-gather | bytes 34816 | tf_op jit(solution)/shard_map/all_gather | solution.py:9
  356.9 3.3 reduce.4
  360.3 1.0 while.30
  361.3 0.9 while.31
  362.2 0.1 fusion.13
  362.4 74.4 %psum.7 = f32[3,512]{0,1:T(8,128)S(1)} all-reduce(f32[3,512]{0,1:T(8,128)S(1)} %fusion.13), channel_id=1, replica_groups=mesh['wide'=16,'narrow'=8] {'wide'}, use_global_device_ids=true, to_apply=%region_18.19 | all-reduce | flops 1536 | bytes 12288 | tf_op jit(solution)/shard_map/psum | solution.py:106
  436.8 0.7 copy.283
  (140 shorter events, 3.3 us)
Async XLA Ops:
  10.5 43.1 %all-to-all-start.1 = ((bf16[128,2,192]{2,1,0:T(2,128)(2,1)}), bf16[128,2,192]{2,1,0:T(2,128)(2,1)S(1)}, u32[]{:S(2)}, u32[]{:S(2)}) async-start(bf16[128,2,192]{2,1,0:T(2,128)(2,1)} %reshape.461), calls=%async_computation.1 | async-start | bytes 262144 | tf_op jit(solution)/shard_map/all_to_all | solution.py:73
  53.5 10.2 %copy-start.9 = (s32[1,512,1]{1,2,0:T(1,128)S(1)}, s32[1,512,1]{1,2,0:T(1,128)}, u32[]{:S(2)}) copy-start(s32[1,512,1]{1,2,0:T(1,128)} %param.13) | copy-start | bytes 6148
  53.5 162.1 %all-to-all-start = ((bf16[128,4,2,48,128]{4,3,2,1,0:T(8,128)(2,1)}), bf16[128,4,2,48,128]{4,3,2,1,0:T(8,128)(2,1)}, u32[]{:S(2)}, u32[]{:S(2)}) async-start(bf16[128,4,2,48,128]{4,3,2,1,0:T(8,128)(2,1)} %broadcast_select_fusion), calls=%async_computation | async-start | bytes 25165824 | tf_op jit(solution)/shard_map/all_to_all | solution.py:66
  67.1 157.4 %copy-start.11 = (bf16[4,128,256]{2,1,0:T(8,128)(2,1)S(1)}, bf16[4,128,256]{2,1,0:T(8,128)(2,1)}, u32[]{:S(2)}) copy-start(bf16[4,128,256]{2,1,0:T(8,128)(2,1)} %param.15) | copy-start | bytes 786436
  224.5 8.1 %copy-start.12 = (bf16[4,4,256]{2,1,0:T(4,128)(2,1)S(1)}, bf16[4,4,256]{2,1,0:T(4,128)(2,1)}, u32[]{:S(2)}) copy-start(bf16[4,4,256]{2,1,0:T(4,128)(2,1)} %param.17) | copy-start | bytes 24580
  270.7 0.7 copy-start.1
  280.4 6.7 %copy-start.3 = (f32[12288]{0:T(1024)S(1)}, f32[12288]{0:T(1024)}, u32[]{:S(2)}) copy-start(f32[12288]{0:T(1024)} %slice_reduce_fusion.3) | copy-start | bytes 147460
  280.4 7.0 %copy-start.4 = (f32[12288]{0:T(1024)S(1)}, f32[12288]{0:T(1024)}, u32[]{:S(2)}) copy-start(f32[12288]{0:T(1024)} %slice_reduce_fusion.2) | copy-start | bytes 147460
  280.4 7.3 %copy-start.7 = (bf16[128,1,2,48]{0,3,2,1:T(8,128)(2,1)S(1)}, bf16[128,1,2,48]{0,3,2,1:T(8,128)(2,1)}, u32[]{:S(2)}) copy-start(bf16[128,1,2,48]{0,3,2,1:T(8,128)(2,1)} %copy.292) | copy-start | bytes 73732
  280.4 7.4 %copy-start.8 = (bf16[128,1,2,48]{0,3,2,1:T(8,128)(2,1)S(1)}, bf16[128,1,2,48]{0,3,2,1:T(8,128)(2,1)}, u32[]{:S(2)}) copy-start(bf16[128,1,2,48]{0,3,2,1:T(8,128)(2,1)} %copy.293) | copy-start | bytes 73732
  280.4 7.6 %copy-start = (f32[3,12288]{1,0:T(4,128)S(1)}, f32[3,12288]{1,0:T(4,128)}, u32[]{:S(2)}) copy-start(f32[3,12288]{1,0:T(4,128)} %fusion.25) | copy-start | bytes 442372
  280.4 10.7 %copy-start.2 = (f32[12288]{0:T(1024)S(1)}, f32[12288]{0:T(1024)}, u32[]{:S(2)}) copy-start(f32[12288]{0:T(1024)} %slice_reduce_fusion.1) | copy-start | bytes 147460
  286.8 5.0 %copy-start.5 = (bf16[128,1,2,48]{0,3,2,1:T(8,128)(2,1)S(1)}, bf16[128,1,2,48]{0,3,2,1:T(8,128)(2,1)}, u32[]{:S(2)}) copy-start(bf16[128,1,2,48]{0,3,2,1:T(8,128)(2,1)} %copy.294) | copy-start | bytes 73732
  286.8 5.0 %copy-start.6 = (bf16[128,1,2,48]{0,3,2,1:T(8,128)(2,1)S(1)}, bf16[128,1,2,48]{0,3,2,1:T(8,128)(2,1)}, u32[]{:S(2)}) copy-start(bf16[128,1,2,48]{0,3,2,1:T(8,128)(2,1)} %copy.295) | copy-start | bytes 73732
  296.3 25.5 %all-to-all-start.2 = ((f32[128,4,2,4]{3,1,2,0:T(4,128)}), f32[128,4,2,4]{3,1,2,0:T(4,128)S(1)}, u32[]{:S(2)}, u32[]{:S(2)}) async-start(f32[128,4,2,4]{3,1,2,0:T(4,128)} %copy.281), calls=%async_computation.2 | async-start | bytes 1048576 | tf_op jit(solution)/shard_map/all_to_all | solution.py:95
  322.1 40.1 %copy-start.10 = (s32[512]{0:T(512)S(1)}, s32[512]{0:T(512)}, u32[]{:S(2)}) copy-start(s32[512]{0:T(512)} %param.14) | copy-start | bytes 6148
where the time goes:
time: 444 us; the launch traced here: 438 us
  waiting for transfers between devices  162 us (36%)
  blocking collectives  108 us (24%)
  matrix products  57.4 us (13%)
  local copies, waits for them, and re-layouts  53.1 us (12%)
  starting transfers between devices  33.3 us (7%)
  other arithmetic  22.1 us (5%)
    all_to_all x1, waiting for transfers between devices, on_device(): lax.all_to_all(send_features.reshape(devices_all, reg_local, capacity, sa...  148 us
    psum x1, blocking collectives, on_device(): return lax.psum(light_term, 'wide')  74.4 us
    all_gather x1, blocking collectives, prefix_2(): everything = lax.all_gather(array, axis)  33.5 us
    dot_general x4, matrix products, on_device(): jnp.dot(hidden, w_mid[region, layer_index], preferred_element_type=jnp.fl...  31.6 us
    dot_general x4, matrix products, on_device(): jnp.einsum('nh,ch->cn', hidden, w_out[region], preferred_element_type=jnp...  25.7 us
    gather x1, local copies, waits for them, and re-layouts, on_device(): send_features = jnp.take(ray_rows, source_row, axis=0)  14.5 us
    all_to_all x1, waiting for transfers between devices, on_device(): lax.all_to_all(partial_here, ('wide', 'narrow'), split_axis=0, concat_axi...  13.5 us
    all_to_all x1, starting transfers between devices, on_device(): lax.all_to_all(partial_here, ('wide', 'narrow'), split_axis=0, concat_axi...  12 us
  transfers between devices with their start and end apart: 3, of which 2 were waited for; matrix products, arithmetic and copies ran while one was open for 8% of the time, Pallas kernels for 0%

commit v1 on v0

--- a/solution.py
+++ b/solution.py
@@ -1,7 +1,46 @@
 import jax
 import jax.numpy as jnp
 from jax import lax
+from jax.experimental import pallas as pl
+from jax.experimental.pallas import tpu as pltpu
 from jax.sharding import PartitionSpec as P
+
+MESH = pl.DeviceIdType.MESH
+F32, BF16, I32 = jnp.float32, jnp.bfloat16, jnp.int32
+ROWS, SAMP, FEAT, HID = 512, 48, 128, 256
+WIDE, NARROW, REG, GROUP = 16, 8, 4, 32
+CAP = 40
+PIECE = 8
+META = 48
+FLAG = 127
+
+SEND_ORDER = ((6, 14, 9, 11, 1, 3, 4, 12, 2, 8, 10), (5, 15, 7, 13))
+CHUNKS = ((0, 6, 14, 9), (11, 1, 3, 4), (12, 2, 8, 10), (5, 15, 7, 13))
+DY_ORDER = (1, 3, 2)
+
+
+def nt(a, b, precision=None):
+    return lax.dot_general(a, b, (((1,), (1,)), ((), ())), precision=precision, preferred_element_type=F32)
+
+
+def tn(a, b, precision=None):
+    return lax.dot_general(a, b, (((0,), (0,)), ((), ())), precision=precision, preferred_element_type=F32)
+
+
+def dot(a, b, precision=None):
+    return jnp.dot(a, b, precision=precision, preferred_element_type=F32)
+
+
+def onehot(rows, lanes_value):
+    return lax.broadcasted_iota(I32, (rows, lanes_value.shape[1]), 0) == lanes_value
+
+
+def within(i, size):
+    return jnp.minimum(jnp.maximum(i, 0), size - 1)
+
+
+def relu(v):
+    return jnp.maximum(v.astype(BF16), 0)
 
 
 def prefix_2(array, axis, combine, identity, reverse):
@@ -33,7 +72,7 @@
     return earlier + later
 
 
-def on_device(samples, spacing, region_ids, directions, w_in, w_mid, w_out):
+def general(samples, spacing, region_ids, directions, w_in, w_mid, w_out):
     wide_size = lax.axis_size("wide")
     narrow_size = lax.axis_size("narrow")
     devices_all = wide_size * narrow_size
@@ -106,6 +145,286 @@
     return lax.psum(light_term, "wide")
 
 
+def render_kernel(samples, spacing, ids, dirs, w_in, w_mid, w_out, out, *scratch):
+    (rows, send, recv0, recv1, recv2, recv3, wi, wm, wo, wp, meta_s, meta_r, pos_v, pos_s, idx_v, idx_s, acc,
+     ret_s, ret_r, fin_s, fin_r, flag_s, flag_r, local_sem, wt_send, wt_recv, fwd_send, meta_ss, meta_rs,
+     data_ss, data_rs, ret_ss, ret_rs, fin_ss, fin_rs, flag_ss, flag_rs) = scratch
+    recv = (recv0, recv1, recv2, recv3)
+    place = {k: (q, s) for q, chunk in enumerate(CHUNKS) for s, k in enumerate(chunk)}
+    wide, nar = lax.axis_index("wide"), lax.axis_index("narrow")
+    z, x = wide // 4, wide % 4
+    y, core = nar // 2, nar % 2
+
+    def group_at(k, sign=1):
+        return ((z + sign * (k // 4) + 4) % 4) * 4 + (x + sign * (k % 4) + 4) % 4
+
+    def wide_at(k, sign=1):
+        return (group_at(k, sign), nar)
+
+    def narrow_at(dy, dc, sign=1):
+        return (wide, ((y + sign * dy + 4) % 4) * 2 + (core + dc) % 2)
+
+    def remote(src, dst, ss, rs, to):
+        return pltpu.make_async_remote_copy(
+            src_ref=src, dst_ref=dst, send_sem=ss, recv_sem=rs, device_id=to, device_id_type=MESH)
+
+    barrier = pltpu.get_barrier_semaphore()
+    for k in range(1, WIDE):
+        pl.semaphore_signal(barrier, inc=1, device_id=wide_at(k), device_id_type=MESH)
+    for t in range(1, NARROW):
+        pl.semaphore_signal(barrier, inc=1, device_id=narrow_at(t // 2, t % 2), device_id_type=MESH)
+
+    here = [pltpu.make_async_copy(samples, rows, local_sem.at[0]),
+            pltpu.make_async_copy(w_in, wi.at[pl.ds(0, REG)], local_sem.at[1]),
+            pltpu.make_async_copy(w_mid, wm.at[pl.ds(0, REG)], local_sem.at[2]),
+            pltpu.make_async_copy(w_out, wo.at[0], local_sem.at[3])]
+    for copy in here:
+        copy.start()
+
+    rid = ids[...]
+    g = jnp.right_shift(rid, 5)
+    nb = jnp.bitwise_and(jnp.right_shift(rid, 2), 7)
+    t = jnp.bitwise_and(jnp.right_shift(nb, 1) - y, 3) * 2 + jnp.bitwise_and(nb + core, 1)
+    r = t * REG + jnp.bitwise_and(rid, 3)
+    ray = lax.broadcasted_iota(I32, (1, ROWS), 1)
+    before = (lax.broadcasted_iota(I32, (ROWS, ROWS), 0) < lax.broadcasted_iota(I32, (ROWS, ROWS), 1)).astype(BF16)
+    of_region = onehot(WIDE * GROUP, g * GROUP + r).astype(F32)
+    a = jnp.sum(of_region * dot(of_region.astype(BF16), before), axis=0, keepdims=True)
+    of_group = onehot(WIDE, g).astype(F32)
+    p = jnp.sum(of_group * dot(of_group.astype(BF16), before), axis=0, keepdims=True)
+    a_int, p_int = a.astype(I32), p.astype(I32)
+    at_place = onehot(128, p_int).astype(BF16)
+    low = nt((of_group * jnp.bitwise_and(ray, 15).astype(F32)).astype(BF16), at_place)
+    high = nt((of_group * jnp.right_shift(ray, 4).astype(F32)).astype(BF16), at_place)
+    idx_v[...] = (low + 16.0 * high).astype(I32)
+    to_smem = pltpu.make_async_copy(idx_v, idx_s, local_sem.at[4])
+    to_smem.start()
+    slot = onehot(128, a_int * GROUP + r).astype(BF16)
+    position = nt((of_group * jnp.minimum(p, CAP - 1.0)).astype(BF16), slot)
+    over = (jnp.max(p, axis=1, keepdims=True) >= CAP).astype(F32)
+    position = jnp.where(lax.broadcasted_iota(I32, (WIDE, 128), 1) == FLAG, over, position)
+    lane = lax.broadcasted_iota(I32, (SAMP, 128), 1)
+    samp = lax.broadcasted_iota(I32, (SAMP, 128), 0)
+    gaps = spacing[...]
+    first = dot(gaps, (lane == samp).astype(BF16)).astype(BF16)
+    second = dot(gaps, (lane == samp + SAMP).astype(BF16)).astype(BF16)
+    gap_slots = dot((of_region * (1.0 - a)).astype(BF16), first) + dot((of_region * a).astype(BF16), second)
+    meta_s[:, 0:GROUP, :] = gap_slots.astype(BF16).reshape(WIDE, GROUP, 128)
+    for w in range(WIDE):
+        meta_s[w, GROUP:META, :] = jnp.broadcast_to(position[w:w + 1], (META - GROUP, 128)).astype(BF16)
+    meta_r[0] = meta_s[wide]
+
+    pl.semaphore_wait(barrier, WIDE - 1 + NARROW - 1)
+
+    def weight_copies(s, to, mine):
+        source = (w_in, w_mid, w_out) if mine else (
+            wi.at[pl.ds((s - 1) * REG, REG)], wm.at[pl.ds((s - 1) * REG, REG)], wo.at[s - 1])
+        target = (wi.at[pl.ds(s * REG, REG)], wm.at[pl.ds(s * REG, REG)], wo.at[s])
+        return [remote(source[i], target[i], wt_send.at[i, s], wt_recv.at[i, s], to) for i in range(3)]
+
+    weights = {1: weight_copies(1, narrow_at(0, 1), True)}
+    for dy in DY_ORDER:
+        weights[2 * dy] = weight_copies(2 * dy, narrow_at(dy, 0, -1), True)
+        weights[2 * dy + 1] = weight_copies(2 * dy + 1, narrow_at(0, 1), False)
+    for s in (1,) + tuple(2 * dy for dy in DY_ORDER):
+        for copy in weights[s]:
+            copy.start()
+
+    metas = {k: remote(meta_s.at[group_at(k)], meta_r.at[k], meta_ss.at[k], meta_rs.at[k], wide_at(k))
+             for order in SEND_ORDER for k in order}
+    for copy in metas.values():
+        copy.start()
+
+    here[0].wait()
+    to_smem.wait()
+
+    def data_copy(k, start, size):
+        q, s = place[k]
+        return remote(send.at[k - 1, pl.ds(start, size)], recv[q].at[pl.ds(s * CAP + start, size)],
+                      data_ss.at[k], data_rs.at[k], wide_at(k))
+
+    for order in SEND_ORDER:
+        def pack(piece, carry, order=order):
+            for k in order:
+                to = group_at(k)
+                for m in range(PIECE):
+                    send[k - 1, piece * PIECE + m] = rows[within(idx_s[to, piece * PIECE + m], ROWS)]
+                data_copy(k, piece * PIECE, PIECE).start()
+            return carry
+
+        lax.fori_loop(0, CAP // PIECE, pack, 0)
+
+    def pack_own(piece, carry):
+        q, s = place[0]
+        for m in range(PIECE):
+            recv[q][s * CAP + piece * PIECE + m] = rows[within(idx_s[wide, piece * PIECE + m], ROWS)]
+        return carry
+
+    lax.fori_loop(0, CAP // PIECE, pack_own, 0)
+
+    for k in range(1, WIDE):
+        metas[k].wait_recv()
+    flag = None
+    for k in range(WIDE):
+        line = meta_r[k, GROUP:META, :].astype(F32)[0:8]
+        pos_v[k] = line.astype(I32)
+        flag = line if flag is None else jnp.maximum(flag, line)
+    to_smem = pltpu.make_async_copy(pos_v, pos_s, local_sem.at[5])
+    to_smem.start()
+    flag_s[...] = flag
+    flags = {s: remote(flag_s, flag_r.at[s], flag_ss.at[s], flag_rs.at[s], narrow_at(s // 2, s % 2))
+             for s in range(1, NARROW)}
+    for copy in flags.values():
+        copy.start()
+
+    for dy in DY_ORDER:
+        for copy in weights[2 * dy]:
+            copy.wait_recv()
+        for copy in weights[2 * dy + 1]:
+            copy.start()
+    for copy in here[1:]:
+        copy.wait()
+    for s in (1, 3, 5, 7):
+        for copy in weights[s]:
+            copy.wait_recv()
+    to_smem.wait()
+
+    def spread(s, carry):
+        lanes = lax.broadcasted_iota(I32, (REG * 4, 128), 1)
+        line = lax.broadcasted_iota(I32, (REG * 4, 128), 0)
+        channel = jnp.bitwise_and(line, 3)
+        for j in range(REG):
+            match = jnp.logical_and(jnp.right_shift(line, 2) == j, lanes == channel * GROUP + s * REG + j)
+            wp[pl.ds((s * REG + j) * HID, HID)] = tn(wo[s], match.astype(BF16)).astype(BF16)
+        return carry
+
+    lax.fori_loop(0, NARROW, spread, 0)
+
+    line = lax.broadcasted_iota(I32, (8 * SAMP, 8 * SAMP), 0)
+    lane = lax.broadcasted_iota(I32, (8 * SAMP, 8 * SAMP), 1)
+    same = jnp.zeros(line.shape, jnp.bool_)
+    for b in range(8):
+        inside = jnp.logical_and(line >= b * SAMP, line < (b + 1) * SAMP)
+        same = jnp.logical_or(same, jnp.logical_and(inside, jnp.logical_and(lane >= b * SAMP, lane < (b + 1) * SAMP)))
+    earlier = jnp.logical_and(same, line < lane).astype(F32)
+    line = lax.broadcasted_iota(I32, (8, 8 * SAMP), 0)
+    lane = lax.broadcasted_iota(I32, (8, 8 * SAMP), 1)
+    pick = jnp.logical_and(lane >= line * SAMP, lane < (line + 1) * SAMP).astype(F32)
+
+    returns = {}
+    for q, chunk in enumerate(CHUNKS):
+        for k in chunk:
+            if k:
+                data_copy(k, 0, CAP).wait_recv()
+        acc[...] = jnp.zeros_like(acc)
+
+        def regions(dy, carry, q=q, chunk=chunk):
+            def rows_of(j):
+                return jnp.concatenate(
+                    [recv[q][s * CAP + within(pos_s[k, 0, ahead * GROUP + dy * 2 * REG + j], CAP)]
+                     for s, k in enumerate(chunk) for ahead in range(2)], axis=0)
+
+            span = range(2 * REG)
+            hidden = [relu(dot(rows_of(j), wi[dy * 2 * REG + j])) for j in span]
+            hidden = [relu(dot(hidden[j], wm[dy * 2 * REG + j, 0])) for j in span]
+            hidden = [relu(dot(hidden[j], wm[dy * 2 * REG + j, 1])) for j in span]
+            acc[...] += dot(jnp.concatenate(hidden, axis=1), wp[pl.ds(dy * 2 * REG * HID, 2 * REG * HID)])
+            return carry
+
+        lax.fori_loop(0, NARROW // 2, regions, 0)
+
+        raw = acc[...].T
+        gap = jnp.concatenate([meta_r[k, 0:GROUP, 0:2 * SAMP].astype(F32) for k in chunk], axis=1)
+        density = raw[0:GROUP]
+        density = jnp.maximum(density, 0.0) + jnp.log1p(jnp.exp(-jnp.abs(density)))
+        optical = density * gap
+        passed = jnp.exp(-dot(optical, earlier, lax.Precision.HIGHEST))
+        series = optical * (1.0 - optical * (1 / 2 - optical * (1 / 6 - optical * (1 / 24 - optical * (1 / 120)))))
+        weight = passed * jnp.where(optical < 0.125, series, 1.0 - jnp.exp(-optical))
+        parts = [weight * jax.nn.sigmoid(raw[(c + 1) * GROUP:(c + 2) * GROUP]) for c in range(3)] + [optical]
+        result = nt(pick, jnp.concatenate(parts, axis=0), lax.Precision.HIGHEST)
+        for s, k in enumerate(chunk):
+            target = ret_s if k else ret_r
+            target[k, 0:2, :] = result[2 * s:2 * s + 2]
+            if k:
+                returns[k] = remote(ret_s.at[k], ret_r.at[k], ret_ss.at[k], ret_rs.at[k], wide_at(k, -1))
+                returns[k].start()
+
+    for k in range(1, WIDE):
+        returns[k].wait_recv()
+    back = jnp.concatenate([ret_r[k, 0:2, :] for k in range(WIDE)], axis=0)
+    offset = jnp.bitwise_and(jnp.right_shift(g, 2) - z, 3) * 4 + jnp.bitwise_and(jnp.bitwise_and(g, 3) - x, 3)
+    found = tn(back, onehot(2 * WIDE, offset * 2 + a_int).astype(F32), lax.Precision.HIGHEST)
+    keep = onehot(GROUP, r).astype(F32)
+    for c in range(4):
+        fin_s[c:c + 1, :] = jnp.sum(found[c * GROUP:(c + 1) * GROUP] * keep, axis=0, keepdims=True)
+    finals = {k: remote(fin_s, fin_r.at[wide], fin_ss.at[k], fin_rs.at[k], wide_at(k)) for k in range(1, WIDE)}
+    for copy in finals.values():
+        copy.start()
+    fin_r[wide] = fin_s[...]
+    for s in range(1, NARROW):
+        flags[s].wait_recv()
+        flag = jnp.maximum(flag, flag_r[s])
+    for k in range(1, WIDE):
+        remote(fin_s, fin_r.at[group_at(k, -1)], fin_ss.at[k], fin_rs.at[k], wide_at(k)).wait_recv()
+
+    depth = [fin_r[s, 3:4, :] for s in range(WIDE)]
+    ahead, behind = [jnp.zeros_like(depth[0])], [jnp.zeros_like(depth[0])]
+    for s in range(WIDE - 1):
+        ahead.append(ahead[-1] + depth[s])
+        behind.append(behind[-1] + depth[WIDE - 1 - s])
+    backward = dirs[...] == 1
+    colour = jnp.zeros((3, ROWS), F32)
+    for s in range(WIDE):
+        light = jnp.exp(-jnp.where(backward, behind[WIDE - 1 - s], ahead[s]))
+        colour = colour + light * fin_r[s, 0:3, :]
+    out[0:3, :] = colour
+    out[3:8, :] = jnp.broadcast_to(flag[0:1, FLAG:FLAG + 1], (5, ROWS))
+
+    for s in range(1, NARROW):
+        for copy in weights[s]:
+            copy.wait_send()
+        flags[s].wait_send()
+    for k in range(1, WIDE):
+        metas[k].wait_send()
+        data_copy(k, 0, CAP).wait_send()
+        returns[k].wait_send()
+        finals[k].wait_send()
+
+
+def render(samples, spacing, ids, dirs, w_in, w_mid, w_out):
+    vmem, smem, dma = pltpu.VMEM, pltpu.SMEM, pltpu.SemaphoreType.DMA
+    regions = NARROW * REG
+    whole, any_place = pl.BlockSpec(memory_space=pltpu.VMEM), pl.BlockSpec(memory_space=pl.ANY)
+    scratch = [vmem((ROWS, SAMP, FEAT), BF16), vmem((WIDE - 1, CAP, SAMP, FEAT), BF16)]
+    scratch += [vmem((len(chunk) * CAP, SAMP, FEAT), BF16) for chunk in CHUNKS]
+    scratch += [
+        vmem((regions, FEAT, HID), BF16), vmem((regions, 2, HID, HID), BF16), vmem((NARROW, REG * 4, HID), BF16),
+        vmem((regions * HID, 128), BF16), vmem((WIDE, META, 128), BF16), vmem((WIDE, META, 128), BF16),
+        vmem((WIDE, 8, 128), I32), smem((WIDE, 8, 128), I32), vmem((WIDE, 128), I32), smem((WIDE, 128), I32),
+        vmem((8 * SAMP, 128), F32), vmem((WIDE, 8, 128), F32), vmem((WIDE, 8, 128), F32),
+        vmem((8, ROWS), F32), vmem((WIDE, 8, ROWS), F32), vmem((8, 128), F32), vmem((NARROW, 8, 128), F32),
+        dma((6,)), dma((3, NARROW)), dma((3, NARROW)), dma((1,)), dma((WIDE,)), dma((WIDE,)), dma((WIDE,)),
+        dma((WIDE,)), dma((WIDE,)), dma((WIDE,)), dma((WIDE,)), dma((WIDE,)), dma((NARROW,)), dma((NARROW,))]
+    return pl.pallas_call(
+        render_kernel,
+        out_shape=jax.ShapeDtypeStruct((8, ROWS), F32),
+        in_specs=[any_place, whole, whole, whole, any_place, any_place, any_place],
+        out_specs=whole,
+        scratch_shapes=scratch,
+        compiler_params=pltpu.CompilerParams(collective_id=0, has_side_effects=True, vmem_limit_bytes=58 * 2**20),
+        name="render",
+    )(samples, spacing, ids, dirs, w_in, w_mid, w_out)
+
+
+def on_device(samples, spacing, region_ids, directions, w_in, w_mid, w_out):
+    args = (samples, spacing, region_ids, directions, w_in, w_mid, w_out)
+    fast = render(
+        samples.reshape(ROWS, SAMP, FEAT), spacing.reshape(ROWS, SAMP), region_ids.reshape(1, ROWS),
+        directions.reshape(1, ROWS), w_in, w_mid, w_out.reshape(REG * 4, HID))
+    return lax.cond(fast[3, 0] > 0, lambda rest: general(*rest), lambda rest: fast[0:3], args)
+
+
 def solution(mesh):
     in_specs = (
         P("wide", "narrow", None, None),

time: 444 us -> 134 us (0.30); the launches traced: 438 us -> 134 us
  waiting for transfers between devices: 162 us -> 0 us
  Pallas kernels: 0 us -> 129 us
  blocking collectives: 108 us -> 0 us
  matrix products: 57.4 us -> 0 us
  local copies, waits for them, and re-layouts: 53.1 us -> 4.26 us
  starting transfers between devices: 33.3 us -> 0 us
  other arithmetic: 22.1 us -> 0 us
    all_to_all x3 -> x0, waiting for transfers between devices: 162 us -> none  [the longest x1 148 us: on_device(): lax.all_to_all(send_features.reshape(devices_all, reg_local, capacity, sa...]
    pallas_call x0 -> x1, Pallas kernels: none -> 129 us  [render(): pl.pallas_call(render_kernel, out_shape=jax.ShapeDtypeStruct((8, ROWS), F...]
    psum x1 -> x0, blocking collectives: 74.4 us -> none  [on_device(): return lax.psum(light_term, 'wide')]
    dot_general x8 -> x0, matrix products: 57.4 us -> none  [the longest x4 31.6 us: on_device(): jnp.dot(hidden, w_mid[region, layer_index], preferred_element_type=jnp.fl...]
    all_gather x1 -> x0, blocking collectives: 33.5 us -> none  [prefix_2(): everything = lax.all_gather(array, axis)]
    all_to_all x3 -> x0, starting transfers between devices: 33.3 us -> none  [the longest x1 12 us: on_device(): lax.all_to_all(partial_here, ('wide', 'narrow'), split_axis=0, concat_axi...]
    gather x3 -> x0, local copies, waits for them, and re-layouts: 18.7 us -> none  [the longest x1 14.5 us: on_device(): send_features = jnp.take(ray_rows, source_row, axis=0)]
    select_n x36 -> x0, other arithmetic: 13 us -> none  [the longest x1 10.9 us: on_device(): send_features = jnp.take(ray_rows, source_row, axis=0)]
  transfers between devices with their start and end apart: 3 -> 0, of which waited for: 2 -> 0; matrix products, arithmetic and copies ran while one was open for 8% -> 0% of each run, Pallas kernels for 0% -> 0%
where the time goes in v1:
time: 134 us
  Pallas kernels  129 us (96%)
  local copies, waits for them, and re-layouts  4.26 us (3%)
    pallas_call x1, Pallas kernels, render(): pl.pallas_call(render_kernel, out_shape=jax.ShapeDtypeStruct((8, ROWS), F...  129 us

profile of v1, /device:TPU:0, one launch (start us, length us, event | category | flops | bytes accessed | tf_op | source)
XLA Modules:
  0.0 133.8 jit_solution(9377010092374543865)
XLA Ops:
  0.0 0.0 copy-start.5
  0.0 0.0 copy-start.10
  0.0 1.6 %copy.294 = bf16[1,512,48]{2,1,0:T(8,128)(2,1)} copy(bf16[1,512,48]{1,2,0:T(8,128)(2,1)} %param.14) | data formatting | bytes 98304 | tf_op args[1]
  1.6 1.3 reshape.418.w_out
  2.9 128.6 %render.1 = f32[8,512]{1,0:T(8,128)S(1)} custom-call(bf16[512,48,128]{2,1,0:T(8,128)(2,1)} %bitcast.167, bf16[512,48]{1,0:T(8,128)(2,1)} %bitcast.178, s32[1,512]{1,0:T(1,128)} %bitcast.182, s32[1,512]{1,0:T(1,128)} %bitcast.188, bf16[4,128,256]{2,1,0:T(8,128)(2,1)} %w_in.1, bf16[4,2,256,256]{3,2,1,0:T(8,128)(2,1)} %w_mid.1, bf16[16,256]{1,0:T(8,128)(2,1)} %reshape.418.w_out), custom_call_target="tpu_custom_call" | custom-call | tf_op jit(solution)/shard_map/render/pallas_call | solution.py:409
  131.5 0.5 slice.152
  132.7 0.0 copy-done.5
  132.7 0.0 copy-done.10
  132.7 0.4 conditional.1
  132.7 0.1 copy.308
  132.9 0.1 copy.306
  133.2 0.0 copy-start.11
  133.2 0.6 copy-done.11
Async XLA Ops:
  0.0 132.7 %copy-start.5 = (bf16[1,512,48]{1,2,0:T(8,128)(2,1)S(1)}, bf16[1,512,48]{1,2,0:T(8,128)(2,1)}, u32[]{:S(2)}) copy-start(bf16[1,512,48]{1,2,0:T(8,128)(2,1)} %param.14) | copy-start | bytes 147460
  0.0 132.7 %copy-start.10 = (s32[1,512,1]{1,2,0:T(1,128)S(1)}, s32[1,512,1]{1,2,0:T(1,128)}, u32[]{:S(2)}) copy-start(s32[1,512,1]{1,2,0:T(1,128)} %param.15) | copy-start | bytes 6148
  133.2 0.6 copy-start.11

commit v2 on v1

v2 whole, which is shorter than its diff:
```python
import jax
import jax.numpy as jnp
from jax import lax
from jax.experimental import pallas as pl
from jax.experimental.pallas import tpu as pltpu
from jax.sharding import PartitionSpec as P

MESH = pl.DeviceIdType.MESH
F32, BF16, I32 = jnp.float32, jnp.bfloat16, jnp.int32
ROWS, SAMP, FEAT, HID = 512, 48, 128, 256
WIDE, NARROW, REG, GROUP = 16, 8, 4, 32
CAP = 40
PIECE = 8
META = 48
FLAG = 127

SEND_ORDER = ((6, 14, 9, 11, 1, 3, 4, 12), (2, 8, 10))
HELD = {0: ((5, 15),), 1: ((7, 13),)}
CHUNKS = ((0, 6, 14, 9), (11, 1, 3, 4), (12, 2, 8, 10), (5, 15), (7, 13))
MOST = 4 * 2 * SAMP


def nt(a, b):
    return lax.dot_general(a, b, (((1,), (1,)), ((), ())), preferred_element_type=F32)


def tn(a, b):
    return lax.dot_general(a, b, (((0,), (0,)), ((), ())), preferred_element_type=F32)


def dot(a, b):
    return jnp.dot(a, b, preferred_element_type=F32)


def halves(v):
    high = v.astype(BF16)
    return jnp.concatenate([high, (v - high.astype(F32)).astype(BF16)], axis=0)


def onehot(rows, lanes_value):
    return lax.broadcasted_iota(I32, (rows, lanes_value.shape[1]), 0) == lanes_value


def within(i, size):
    return jnp.minimum(jnp.maximum(i, 0), size - 1)


def relu(v):
    return jnp.maximum(v.astype(BF16), 0)


def prefix_2(array, axis, combine, identity, reverse):
    count, position = (lax.axis_size(axis), lax.axis_index(axis))
    everything = lax.all_gather(array, axis)
    start = jnp.broadcast_to(jnp.asarray(identity, array.dtype), array.shape)

    def hop(k, before):
        at = count - 1 - k if reverse else k
        reached = at > position if reverse else at < position
        new = combine(before, everything[at])
        return jnp.where(reached, new, before)

    return lax.fori_loop(0, count, hop, start)


def composite(raw_out, spacing_part):
    density = jax.nn.softplus(raw_out[0])
    colours = jax.nn.sigmoid(raw_out[1:4])
    optical = density * spacing_part.astype(jnp.float32)
    before_sum = jnp.cumsum(optical, axis=-1) - optical
    sample_weight = jnp.exp(-before_sum) * -jnp.expm1(-optical)
    seg_colour = jnp.sum(sample_weight * colours, axis=-1)
    seg_depth = jnp.sum(optical, axis=-1)
    return jnp.stack([seg_colour[0], seg_colour[1], seg_colour[2], seg_depth], axis=-1)


def accumulate(earlier, later):
    return earlier + later


def general(samples, spacing, region_ids, directions, w_in, w_mid, w_out):
    wide_size = lax.axis_size("wide")
    narrow_size = lax.axis_size("narrow")
    devices_all = wide_size * narrow_size
    reg_local = w_in.shape[0]
    ray_local = samples.shape[1]
    sample_len = samples.shape[2]
    width_in = samples.shape[3]
    region_all = reg_local * devices_all
    capacity = max(2, 2 * ray_local // region_all)
    slot_total = region_all * capacity
    region_row = region_ids.reshape(ray_local)
    matches = region_row[:, None] == region_row[None, :]
    positions = jnp.arange(ray_local, dtype=jnp.int32)
    earlier = positions[None, :] < positions[:, None]
    arrival = jnp.sum(jnp.logical_and(matches, earlier), axis=1)
    slot_index = region_row * capacity + arrival
    source_row = jnp.full((slot_total,), ray_local, jnp.int32).at[slot_index].set(positions)
    ray_rows = jnp.concatenate(
        [
            samples.reshape(ray_local, sample_len, width_in),
            jnp.zeros((1, sample_len, width_in), samples.dtype),
        ],
        axis=0,
    )
    gap_rows = jnp.concatenate(
        [spacing.reshape(ray_local, sample_len), jnp.zeros((1, sample_len), spacing.dtype)], axis=0
    )
    send_features = jnp.take(ray_rows, source_row, axis=0)
    send_spacing = jnp.take(gap_rows, source_row, axis=0)
    features = lax.all_to_all(
        send_features.reshape(devices_all, reg_local, capacity, sample_len, width_in),
        ("wide", "narrow"),
        split_axis=0,
        concat_axis=0,
        tiled=True,
    )
    spacing_part = lax.all_to_all(
        send_spacing.reshape(devices_all, reg_local, capacity, sample_len),
        ("wide", "narrow"),
        split_axis=0,
        concat_axis=0,
        tiled=True,
    )
    results = []
    for region in range(reg_local):
        inputs = features[:, region].reshape(-1, width_in)
        hidden = jax.nn.relu(
            jnp.dot(inputs, w_in[region], preferred_element_type=jnp.float32)
        ).astype(jnp.bfloat16)
        for layer_index in range(w_mid.shape[1]):
            hidden = jax.nn.relu(
                jnp.dot(hidden, w_mid[region, layer_index], preferred_element_type=jnp.float32)
            ).astype(jnp.bfloat16)
        raw_out = jnp.einsum("nh,ch->cn", hidden, w_out[region], preferred_element_type=jnp.float32)
        part_gap = spacing_part[:, region]
        raw_out = raw_out.reshape((4,) + part_gap.shape)
        results.append(composite(raw_out, part_gap))
    partial_here = jnp.stack(results, axis=1)
    returned = lax.all_to_all(
        partial_here, ("wide", "narrow"), split_axis=0, concat_axis=0, tiled=True
    )
    mine = jnp.take(returned.reshape(slot_total, 4), slot_index, axis=0)
    seg_depth = mine[:, 3]
    zero_depth = jnp.zeros_like(seg_depth)
    ahead = prefix_2(seg_depth, "wide", accumulate, zero_depth, False)
    behind = prefix_2(seg_depth, "wide", accumulate, zero_depth, True)
    prefix = jnp.where(directions == 1, behind, ahead)
    light = jnp.exp(-prefix)
    light_term = (light[:, None] * mine[:, :3]).T
    return lax.psum(light_term, "wide")


def render_kernel(samples, spacing, ids, dirs, w_in, w_mid, w_out, out, over_out, *scratch):
    (rows, send, recv0, recv1, recv2, recv3, recv4, wi, wm, wo, wp, meta_s, meta_r, pos_v, pos_s, idx_v, idx_s, acc,
     earlier, pick, where_row, keep, ret_s, ret_r, fin_s, fin_r, flag_s, flag_r, local_sem, wt_send, wt_recv,
     meta_ss, meta_rs, data_ss, data_rs, ret_ss, ret_rs, fin_ss, fin_rs, flag_ss, flag_rs) = scratch
    recv = (recv0, recv1, recv2, recv3, recv4)
    place = {k: (q, s) for q, chunk in enumerate(CHUNKS) for s, k in enumerate(chunk)}
    wide, nar = lax.axis_index("wide"), lax.axis_index("narrow")
    z, x = wide // 4, wide % 4
    y, core = nar // 2, nar % 2

    def group_at(k, sign=1):
        return ((z + sign * (k // 4) + 4) % 4) * 4 + (x + sign * (k % 4) + 4) % 4

    def wide_at(k, sign=1):
        return (group_at(k, sign), nar)

    def narrow_at(dy, dc):
        return (wide, ((y + dy + 4) % 4) * 2 + (core + dc) % 2)

    def remote(src, dst, ss, rs, to):
        return pltpu.make_async_remote_copy(
            src_ref=src, dst_ref=dst, send_sem=ss, recv_sem=rs, device_id=to, device_id_type=MESH)

    barrier = pltpu.get_barrier_semaphore()
    for k in range(1, WIDE):
        pl.semaphore_signal(barrier, inc=1, device_id=wide_at(k), device_id_type=MESH)
    for t in range(1, NARROW):
        pl.semaphore_signal(barrier, inc=1, device_id=narrow_at(t // 2, t % 2), device_id_type=MESH)

    quarter = ROWS // 4
    own_rows = [pltpu.make_async_copy(samples.at[pl.ds(i * quarter, quarter)], rows.at[pl.ds(i * quarter, quarter)],
                                      local_sem.at[i]) for i in range(4)]
    own_weights = [pltpu.make_async_copy(w_in, wi.at[pl.ds(0, REG)], local_sem.at[4]),
                   pltpu.make_async_copy(w_mid, wm.at[pl.ds(0, REG)], local_sem.at[5]),
                   pltpu.make_async_copy(w_out, wo.at[0], local_sem.at[6])]
    for copy in own_rows + own_weights:
        copy.start()

    rid = ids[...]
    g = jnp.right_shift(rid, 5)
    ray = lax.broadcasted_iota(I32, (1, ROWS), 1)
    before = (lax.broadcasted_iota(I32, (ROWS, ROWS), 0) < lax.broadcasted_iota(I32, (ROWS, ROWS), 1)).astype(BF16)
    of_group = onehot(WIDE, g).astype(F32)
    p = jnp.sum(of_group * dot(of_group.astype(BF16), before), axis=0, keepdims=True)
    at_place = onehot(128, p.astype(I32)).astype(BF16)
    low = of_group * jnp.bitwise_and(ray, 15).astype(F32)
    high = of_group * jnp.right_shift(ray, 4).astype(F32)
    source = nt(jnp.concatenate([low, high], axis=0).astype(BF16), at_place)
    idx_v[...] = (source[0:WIDE] + 16.0 * source[WIDE:2 * WIDE]).astype(I32)
    to_smem = pltpu.make_async_copy(idx_v, idx_s, local_sem.at[7])
    to_smem.start()

    pl.semaphore_wait(barrier, WIDE - 1 + NARROW - 1)

    half = REG // 2

    def weight_copies(s, to, taken_from=None):
        copies = []
        for h in range(2):
            for ref, own in ((wi, w_in), (wm, w_mid)):
                src = own.at[pl.ds(h * half, half)] if taken_from is None else ref.at[pl.ds(taken_from * REG + h * half, half)]
                i = 2 * h + (0 if ref is wi else 1)
                copies.append(remote(src, ref.at[pl.ds(s * REG + h * half, half)], wt_send.at[i, s], wt_recv.at[i, s], to))
        src = w_out if taken_from is None else wo.at[taken_from]
        return copies + [remote(src, wo.at[s], wt_send.at[4, s], wt_recv.at[4, s], to)]

    weights = {1: weight_copies(1, narrow_at(0, 1)), 2: weight_copies(2, narrow_at(-1, 0)),
               6: weight_copies(6, narrow_at(1, 0)), 3: weight_copies(3, narrow_at(0, 1), 2),
               7: weight_copies(7, narrow_at(0, 1), 6), 5: weight_copies(5, narrow_at(0, 1), 4)}
    weights[4] = weight_copies(4, narrow_at(-1, 0), 2)[0:2] + weight_copies(4, narrow_at(1, 0), 6)[2:4]
    weights[4] += weight_copies(4, narrow_at(2, 0))[4:5]
    first, second, last = slice(0, 2), slice(2, 4), slice(4, 5)

    def start(s, part):
        for copy in weights[s][part]:
            copy.start()

    def arrived(s, part):
        for copy in weights[s][part]:
            copy.wait_recv()

    for s, part in ((2, last), (6, last), (4, last), (2, first), (6, second), (2, second), (6, first),
                    (1, last), (1, first), (1, second)):
        start(s, part)

    for copy in own_rows:
        copy.wait()
    to_smem.wait()

    def data_copy(k, begin, size):
        q, s = place[k]
        return remote(send.at[k - 1, pl.ds(begin, size)], recv[q].at[pl.ds(s * CAP + begin, size)],
                      data_ss.at[k], data_rs.at[k], wide_at(k))

    def pack(piece, order):
        for k in order:
            to = group_at(k)
            for m in range(PIECE):
                send[k - 1, piece * PIECE + m] = rows[within(idx_s[to, piece * PIECE + m], ROWS)]
            data_copy(k, piece * PIECE, PIECE).start()

    pack(0, SEND_ORDER[0])

    nb = jnp.bitwise_and(jnp.right_shift(rid, 2), 7)
    t = jnp.bitwise_and(jnp.right_shift(nb, 1) - y, 3) * 2 + jnp.bitwise_and(nb + core, 1)
    r = t * REG + jnp.bitwise_and(rid, 3)
    of_region = onehot(WIDE * GROUP, g * GROUP + r).astype(BF16)
    a = jnp.sum(of_region.astype(F32) * dot(of_region, before), axis=0, keepdims=True)
    a_int = a.astype(I32)
    slot = onehot(128, a_int * GROUP + r).astype(BF16)
    position = nt((of_group * jnp.minimum(p, CAP - 1.0)).astype(BF16), slot)
    over = (jnp.max(p, axis=1, keepdims=True) >= CAP).astype(F32)
    position = jnp.where(lax.broadcasted_iota(I32, (WIDE, 128), 1) == FLAG, over, position)
    gaps = spacing[...].astype(F32)
    gaps = jnp.concatenate([gaps * (1.0 - a), gaps * a, jnp.zeros((128 - 2 * SAMP, ROWS), F32)], axis=0).astype(BF16)
    meta_s[:, 0:GROUP, :] = nt(of_region, gaps).astype(BF16).reshape(WIDE, GROUP, 128)
    for w in range(WIDE):
        meta_s[w, GROUP:META, :] = jnp.broadcast_to(position[w:w + 1], (META - GROUP, 128)).astype(BF16)
    meta_r[0] = meta_s[wide]
    metas = {k: remote(meta_s.at[group_at(k)], meta_r.at[k], meta_ss.at[k], meta_rs.at[k], wide_at(k))
             for k in range(1, WIDE)}
    for copy in metas.values():
        copy.start()

    def pack_all(order, begin=0):
        def step(piece, carry):
            pack(piece, order)
            return carry

        lax.fori_loop(begin, CAP // PIECE, step, 0)

    for i, order in enumerate(SEND_ORDER):
        pack_all(order, 1 if i == 0 else 0)

    def pack_own(piece, carry):
        q, s = place[0]
        for m in range(PIECE):
            recv[q][s * CAP + piece * PIECE + m] = rows[within(idx_s[wide, piece * PIECE + m], ROWS)]
        return carry

    lax.fori_loop(0, CAP // PIECE, pack_own, 0)

    offset = jnp.bitwise_and(jnp.right_shift(g, 2) - z, 3) * 4 + jnp.bitwise_and(jnp.bitwise_and(g, 3) - x, 3)
    came = onehot(2 * WIDE, offset * 2 + a_int).astype(F32)
    where_row[...] = jnp.concatenate([came, came], axis=0).astype(BF16)
    keep[...] = onehot(GROUP, r).astype(F32)
    line = lax.broadcasted_iota(I32, (MOST, MOST), 0)
    lane = lax.broadcasted_iota(I32, (MOST, MOST), 1)
    same = jnp.zeros((MOST, MOST), jnp.bool_)
    for b in range(MOST // SAMP):
        ends = (b * SAMP, (b + 1) * SAMP)
        same = jnp.logical_or(same, jnp.logical_and(jnp.logical_and(line >= ends[0], line < ends[1]),
                                                    jnp.logical_and(lane >= ends[0], lane < ends[1])))
    earlier[...] = jnp.logical_and(same, line < lane).astype(BF16)
    line = lax.broadcasted_iota(I32, (16, MOST), 0)
    lane = lax.broadcasted_iota(I32, (16, MOST), 1)
    pick[...] = jnp.logical_and(lane >= line * SAMP, lane < (line + 1) * SAMP).astype(BF16)

    for k in range(1, WIDE):
        metas[k].wait_recv()
    flag = None
    for k in range(WIDE):
        line = meta_r[k, GROUP:META, :].astype(F32)[0:8]
        pos_v[k] = line.astype(I32)
        flag = line if flag is None else jnp.maximum(flag, line)
    to_smem = pltpu.make_async_copy(pos_v, pos_s, local_sem.at[8])
    to_smem.start()
    flag_s[...] = flag
    flags = {s: remote(flag_s, flag_r.at[s], flag_ss.at[s], flag_rs.at[s], narrow_at(s // 2, s % 2))
             for s in range(1, NARROW)}
    for copy in flags.values():
        copy.start()

    for s in (2, 6, 4):
        arrived(s, last)
        start(s + 1, last)
    own_weights[2].wait()
    for s in (1, 3, 7, 5):
        arrived(s, last)

    def spread(s, carry):
        lanes = lax.broadcasted_iota(I32, (REG * 4, 128), 1)
        line = lax.broadcasted_iota(I32, (REG * 4, 128), 0)
        channel = jnp.bitwise_and(line, 3)
        heads = wo[s].astype(F32).reshape(REG * 4, HID).astype(BF16)
        for j in range(REG):
            match = jnp.logical_and(jnp.right_shift(line, 2) == j, lanes == channel * GROUP + s * REG + j)
            wp[pl.ds((s * REG + j) * HID, HID)] = tn(heads, match.astype(BF16)).astype(BF16)
        return carry

    lax.fori_loop(0, NARROW, spread, 0)

    arrived(2, first), start(4, first), start(3, first)
    arrived(6, second), start(4, second), start(7, second)
    arrived(2, second), start(3, second)
    arrived(6, first), start(7, first)
    own_weights[0].wait(), own_weights[1].wait()
    for s in (1, 3, 7):
        arrived(s, first), arrived(s, second)
    arrived(4, first), start(5, first)
    arrived(4, second), start(5, second)
    arrived(5, first), arrived(5, second)
    to_smem.wait()

    returns = {}
    for q, chunk in enumerate(CHUNKS):
        size = len(chunk) * 2 * SAMP
        for k in chunk:
            if k:
                data_copy(k, 0, CAP).wait_recv()
        for order in HELD.get(q, ()):
            pack_all(order)
        acc[...] = jnp.zeros_like(acc)

        def regions(dy, carry, q=q, chunk=chunk, size=size):
            def rows_of(j):
                return jnp.concatenate(
                    [recv[q][s * CAP + within(pos_s[k, 0, ahead * GROUP + dy * 2 * REG + j], CAP)]
                     for s, k in enumerate(chunk) for ahead in range(2)], axis=0)

            span = range(2 * REG)
            hidden = [relu(dot(rows_of(j), wi[dy * 2 * REG + j])) for j in span]
            hidden = [relu(dot(hidden[j], wm[dy * 2 * REG + j, 0])) for j in span]
            hidden = [relu(dot(hidden[j], wm[dy * 2 * REG + j, 1])) for j in span]
            acc[0:size] += dot(jnp.concatenate(hidden, axis=1), wp[pl.ds(dy * 2 * REG * HID, 2 * REG * HID)])
            return carry

        lax.fori_loop(0, NARROW // 2, regions, 0)

        raw = acc[0:size].T
        gap = jnp.concatenate([meta_r[k, 0:GROUP, 0:2 * SAMP].astype(F32) for k in chunk], axis=1)
        density = raw[0:GROUP]
        density = jnp.maximum(density, 0.0) + jnp.log1p(jnp.exp(-jnp.abs(density)))
        optical = density * gap
        sums = dot(halves(optical), earlier[0:size, 0:size])
        passed = jnp.exp(-(sums[0:GROUP] + sums[GROUP:2 * GROUP]))
        series = optical * (1.0 - optical * (1 / 2 - optical * (1 / 6 - optical * (1 / 24 - optical * (1 / 120)))))
        weight = passed * jnp.where(optical < 0.125, series, 1.0 - jnp.exp(-optical))
        parts = [weight * jax.nn.sigmoid(raw[(c + 1) * GROUP:(c + 2) * GROUP]) for c in range(3)] + [optical]
        result = nt(pick[:, 0:size], halves(jnp.concatenate(parts, axis=0)))
        result = result[:, 0:128] + result[:, 128:256]
        for s, k in enumerate(chunk):
            target = ret_s if k else ret_r
            target[k, 0:2, :] = result[2 * s:2 * s + 2]
            if k:
                returns[k] = remote(ret_s.at[k], ret_r.at[k], ret_ss.at[k], ret_rs.at[k], wide_at(k, -1))
                returns[k].start()

    for k in range(1, WIDE):
        returns[k].wait_recv()
    back = jnp.concatenate([ret_r[k, 0:2, :] for k in range(WIDE)], axis=0)
    found = tn(halves(back), where_row[...])
    for c in range(4):
        fin_s[c:c + 1, :] = jnp.sum(found[c * GROUP:(c + 1) * GROUP] * keep[...], axis=0, keepdims=True)
    finals = {k: remote(fin_s, fin_r.at[wide], fin_ss.at[k], fin_rs.at[k], wide_at(k)) for k in range(1, WIDE)}
    for copy in finals.values():
        copy.start()
    fin_r[wide] = fin_s[...]
    for s in range(1, NARROW):
        flags[s].wait_recv()
        flag = jnp.maximum(flag, flag_r[s])
    over_out[...] = jnp.broadcast_to(flag[0:1, FLAG:FLAG + 1], (1, 128))
    for s in range(1, NARROW):
        for copy in weights[s]:
            copy.wait_send()
        flags[s].wait_send()
    for k in range(1, WIDE):
        metas[k].wait_send()
        data_copy(k, 0, CAP).wait_send()
        returns[k].wait_send()
    for k in range(1, WIDE):
        remote(fin_s, fin_r.at[group_at(k, -1)], fin_ss.at[k], fin_rs.at[k], wide_at(k)).wait_recv()

    depth = [fin_r[s, 3:4, :] for s in range(WIDE)]
    ahead, behind = [jnp.zeros_like(depth[0])], [jnp.zeros_like(depth[0])]
    for s in range(WIDE - 1):
        ahead.append(ahead[-1] + depth[s])
        behind.append(behind[-1] + depth[WIDE - 1 - s])
    backward = dirs[...] == 1
    colour = jnp.zeros((3, ROWS), F32)
    for s in range(WIDE):
        light = jnp.exp(-jnp.where(backward, behind[WIDE - 1 - s], ahead[s]))
        colour = colour + light * fin_r[s, 0:3, :]
    out[...] = colour
    for k in range(1, WIDE):
        finals[k].wait_send()


def render(samples, spacing, ids, dirs, w_in, w_mid, w_out):
    vmem, smem, dma = pltpu.VMEM, pltpu.SMEM, pltpu.SemaphoreType.DMA
    regions = NARROW * REG
    whole, any_place = pl.BlockSpec(memory_space=pltpu.VMEM), pl.BlockSpec(memory_space=pl.ANY)
    scratch = [vmem((ROWS, SAMP, FEAT), BF16), vmem((WIDE - 1, CAP, SAMP, FEAT), BF16)]
    scratch += [vmem((len(chunk) * CAP, SAMP, FEAT), BF16) for chunk in CHUNKS]
    scratch += [
        vmem((regions, FEAT, HID), BF16), vmem((regions, 2, HID, HID), BF16), vmem((NARROW, REG, 4, HID), BF16),
        vmem((regions * HID, 128), BF16), vmem((WIDE, META, 128), BF16), vmem((WIDE, META, 128), BF16),
        vmem((WIDE, 8, 128), I32), smem((WIDE, 8, 128), I32), vmem((WIDE, 128), I32), smem((WIDE, 128), I32),
        vmem((MOST, 128), F32), vmem((MOST, MOST), BF16), vmem((16, MOST), BF16), vmem((4 * WIDE, ROWS), BF16),
        vmem((GROUP, ROWS), F32), vmem((WIDE, 8, 128), F32), vmem((WIDE, 8, 128), F32),
        vmem((8, ROWS), F32), vmem((WIDE, 8, ROWS), F32), vmem((8, 128), F32), vmem((NARROW, 8, 128), F32),
        dma((9,)), dma((5, NARROW)), dma((5, NARROW)), dma((WIDE,)), dma((WIDE,)), dma((WIDE,)),
        dma((WIDE,)), dma((WIDE,)), dma((WIDE,)), dma((WIDE,)), dma((WIDE,)), dma((NARROW,)), dma((NARROW,))]
    return pl.pallas_call(
        render_kernel,
        out_shape=(jax.ShapeDtypeStruct((3, ROWS), F32), jax.ShapeDtypeStruct((1, 128), F32)),
        in_specs=[any_place, whole, whole, whole, any_place, any_place, any_place],
        out_specs=(whole, whole),
        scratch_shapes=scratch,
        compiler_params=pltpu.CompilerParams(collective_id=0, has_side_effects=True, vmem_limit_bytes=58 * 2**20),
        name="render",
    )(samples, spacing, ids, dirs, w_in, w_mid, w_out)


def on_device(samples, spacing, region_ids, directions, w_in, w_mid, w_out):
    args = (samples, spacing, region_ids, directions, w_in, w_mid, w_out)
    fast, over = render(
        samples.reshape(ROWS, SAMP, FEAT), spacing.reshape(ROWS, SAMP).T, region_ids.reshape(1, ROWS),
        directions.reshape(1, ROWS), w_in, w_mid, w_out)
    return lax.cond(over[0, 0] > 0, lambda rest: general(*rest), lambda rest: fast, args)


def solution(mesh):
    in_specs = (
        P("wide", "narrow", None, None),
        P("wide", "narrow", None),
        P("wide", "narrow", None),
        P("narrow"),
        P(("wide", "narrow"), None, None),
        P(("wide", "narrow"), None, None, None),
        P(("wide", "narrow"), None, None),
    )
    out_specs = P(None, "narrow")
    return jax.shard_map(
        on_device, mesh=mesh, in_specs=in_specs, out_specs=out_specs, check_vma=False
    )
```

time: 134 us -> 122 us (0.910)
  Pallas kernels: 129 us -> 120 us
  local copies, waits for them, and re-layouts: 4.26 us -> 0.61 us
    pallas_call x1, Pallas kernels: 129 us -> 120 us  [render(): pl.pallas_call(render_kernel, out_shape=(jax.ShapeDtypeStruct((3, ROWS),...]
    unnamed x7 -> x5, local copies, waits for them, and re-layouts: 2.21 us -> 0.61 us
where the time goes in v2:
time: 122 us
  Pallas kernels  120 us (98%)
    pallas_call x1, Pallas kernels, render(): pl.pallas_call(render_kernel, out_shape=(jax.ShapeDtypeStruct((3, ROWS),...  120 us

profile of v2, /device:TPU:0, one launch (start us, length us, event | category | flops | bytes accessed | tf_op | source)
XLA Modules:
  0.0 121.7 jit_solution(1426462295639184416)
XLA Ops:
  0.0 0.0 copy-start.2
  0.0 0.0 copy-start.10
  0.0 120.2 %render.1 = (f32[3,512]{1,0:T(4,128)S(1)}, f32[1,128]{1,0:T(1,128)}) custom-call(bf16[512,48,128]{2,1,0:T(8,128)(2,1)} %bitcast.169, bf16[48,512]{1,0:T(8,128)(2,1)} %bitcast.182, s32[1,512]{1,0:T(1,128)} %bitcast.183, s32[1,512]{1,0:T(1,128)} %bitcast.189, bf16[4,128,256]{2,1,0:T(8,128)(2,1)} %w_in.1, bf16[4,2,256,256]{3,2,1,0:T(8,128)(2,1)} %w_mid.1, ...), custom_call_target="tpu_custom_call" | custom-call | tf_op jit(solution)/shard_map/render/pallas_call | solution.py:457
  120.9 0.0 copy-done.2
  120.9 0.0 copy-done.10
  120.9 0.2 conditional.1
  121.1 0.6 copy.359
Async XLA Ops:
  0.0 120.9 %copy-start.2 = (bf16[1,512,48]{1,2,0:T(8,128)(2,1)S(1)}, bf16[1,512,48]{1,2,0:T(8,128)(2,1)}, u32[]{:S(2)}) copy-start(bf16[1,512,48]{1,2,0:T(8,128)(2,1)} %param.14) | copy-start | bytes 147460
  0.0 120.9 %copy-start.10 = (s32[1,512,1]{1,2,0:T(1,128)S(1)}, s32[1,512,1]{1,2,0:T(1,128)}, u32[]{:S(2)}) copy-start(s32[1,512,1]{1,2,0:T(1,128)} %param.15) | copy-start | bytes 6148

commit v3 on v2

--- a/solution.py
+++ b/solution.py
@@ -11,7 +11,6 @@
 WIDE, NARROW, REG, GROUP = 16, 8, 4, 32
 CAP = 40
 PIECE = 8
-META = 48
 FLAG = 127
 
 SEND_ORDER = ((6, 14, 9, 11, 1, 3, 4, 12), (2, 8, 10))
@@ -152,17 +151,19 @@
 
 
 def render_kernel(samples, spacing, ids, dirs, w_in, w_mid, w_out, out, over_out, *scratch):
-    (rows, send, recv0, recv1, recv2, recv3, recv4, wi, wm, wo, wp, meta_s, meta_r, pos_v, pos_s, idx_v, idx_s, acc,
+    rows, send, *recv = scratch[0:2 + len(CHUNKS)]
+    (wi, wm, wo, wp, meta_s, meta_r, pos_t, pos_v, pos_s, idx_v, idx_s, acc,
      earlier, pick, where_row, keep, ret_s, ret_r, fin_s, fin_r, flag_s, flag_r, local_sem, wt_send, wt_recv,
-     meta_ss, meta_rs, data_ss, data_rs, ret_ss, ret_rs, fin_ss, fin_rs, flag_ss, flag_rs) = scratch
-    recv = (recv0, recv1, recv2, recv3, recv4)
+     meta_ss, meta_rs, pos_ss, pos_rs, data_ss, data_rs, ret_ss, ret_rs, fin_ss, fin_rs, flag_ss, flag_rs) = scratch[2 + len(CHUNKS):]
     place = {k: (q, s) for q, chunk in enumerate(CHUNKS) for s, k in enumerate(chunk)}
     wide, nar = lax.axis_index("wide"), lax.axis_index("narrow")
     z, x = wide // 4, wide % 4
     y, core = nar // 2, nar % 2
 
+    way = 1 - 2 * core
+
     def group_at(k, sign=1):
-        return ((z + sign * (k // 4) + 4) % 4) * 4 + (x + sign * (k % 4) + 4) % 4
+        return ((z + sign * way * (k // 4) + 4) % 4) * 4 + (x + sign * way * (k % 4) + 4) % 4
 
     def wide_at(k, sign=1):
         return (group_at(k, sign), nar)
@@ -232,10 +233,6 @@
         for copy in weights[s][part]:
             copy.wait_recv()
 
-    for s, part in ((2, last), (6, last), (4, last), (2, first), (6, second), (2, second), (6, first),
-                    (1, last), (1, first), (1, second)):
-        start(s, part)
-
     for copy in own_rows:
         copy.wait()
     to_smem.wait()
@@ -253,6 +250,9 @@
             data_copy(k, piece * PIECE, PIECE).start()
 
     pack(0, SEND_ORDER[0])
+    for s, part in ((2, last), (6, last), (4, last), (2, first), (6, second), (2, second), (6, first),
+                    (1, last), (1, first), (1, second)):
+        start(s, part)
 
     nb = jnp.bitwise_and(jnp.right_shift(rid, 2), 7)
     t = jnp.bitwise_and(jnp.right_shift(nb, 1) - y, 3) * 2 + jnp.bitwise_and(nb + core, 1)
@@ -266,14 +266,18 @@
     position = jnp.where(lax.broadcasted_iota(I32, (WIDE, 128), 1) == FLAG, over, position)
     gaps = spacing[...].astype(F32)
     gaps = jnp.concatenate([gaps * (1.0 - a), gaps * a, jnp.zeros((128 - 2 * SAMP, ROWS), F32)], axis=0).astype(BF16)
-    meta_s[:, 0:GROUP, :] = nt(of_region, gaps).astype(BF16).reshape(WIDE, GROUP, 128)
+    meta_s[...] = nt(of_region, gaps).astype(BF16).reshape(WIDE, GROUP, 128)
     for w in range(WIDE):
-        meta_s[w, GROUP:META, :] = jnp.broadcast_to(position[w:w + 1], (META - GROUP, 128)).astype(BF16)
+        pos_t[w] = position[w:w + 1].astype(I32)
     meta_r[0] = meta_s[wide]
+    pos_v[0] = pos_t[wide]
     metas = {k: remote(meta_s.at[group_at(k)], meta_r.at[k], meta_ss.at[k], meta_rs.at[k], wide_at(k))
              for k in range(1, WIDE)}
-    for copy in metas.values():
-        copy.start()
+    places = {k: remote(pos_t.at[group_at(k)], pos_v.at[k], pos_ss.at[k], pos_rs.at[k], wide_at(k))
+              for k in range(1, WIDE)}
+    for k in range(1, WIDE):
+        metas[k].start()
+        places[k].start()
 
     def pack_all(order, begin=0):
         def step(piece, carry):
@@ -293,7 +297,7 @@
 
     lax.fori_loop(0, CAP // PIECE, pack_own, 0)
 
-    offset = jnp.bitwise_and(jnp.right_shift(g, 2) - z, 3) * 4 + jnp.bitwise_and(jnp.bitwise_and(g, 3) - x, 3)
+    offset = jnp.bitwise_and(way * (jnp.right_shift(g, 2) - z), 3) * 4 + jnp.bitwise_and(way * (jnp.bitwise_and(g, 3) - x), 3)
     came = onehot(2 * WIDE, offset * 2 + a_int).astype(F32)
     where_row[...] = jnp.concatenate([came, came], axis=0).astype(BF16)
     keep[...] = onehot(GROUP, r).astype(F32)
@@ -311,13 +315,12 @@
 
     for k in range(1, WIDE):
         metas[k].wait_recv()
-    flag = None
-    for k in range(WIDE):
-        line = meta_r[k, GROUP:META, :].astype(F32)[0:8]
-        pos_v[k] = line.astype(I32)
-        flag = line if flag is None else jnp.maximum(flag, line)
+        places[k].wait_recv()
     to_smem = pltpu.make_async_copy(pos_v, pos_s, local_sem.at[8])
     to_smem.start()
+    flag = pos_v[0]
+    for k in range(1, WIDE):
+        flag = jnp.maximum(flag, pos_v[k])
     flag_s[...] = flag
     flags = {s: remote(flag_s, flag_r.at[s], flag_ss.at[s], flag_rs.at[s], narrow_at(s // 2, s % 2))
              for s in range(1, NARROW)}
@@ -348,11 +351,8 @@
     arrived(2, second), start(3, second)
     arrived(6, first), start(7, first)
     own_weights[0].wait(), own_weights[1].wait()
-    for s in (1, 3, 7):
-        arrived(s, first), arrived(s, second)
-    arrived(4, first), start(5, first)
-    arrived(4, second), start(5, second)
-    arrived(5, first), arrived(5, second)
+    for part in (first, second):
+        arrived(1, part)
     to_smem.wait()
 
     returns = {}
@@ -365,7 +365,23 @@
             pack_all(order)
         acc[...] = jnp.zeros_like(acc)
 
-        def regions(dy, carry, q=q, chunk=chunk, size=size):
+        def regions(i, carry, q=q, chunk=chunk, size=size):
+            dy = i + (i // 2) * (1 - 2 * (i % 2))
+            if q == 0:
+                @pl.when(i == 1)
+                def _():
+                    arrived(3, first), arrived(3, second)
+
+                @pl.when(i == 2)
+                def _():
+                    arrived(4, first), start(5, first)
+                    arrived(4, second), start(5, second)
+                    arrived(7, first), arrived(7, second)
+
+                @pl.when(i == 3)
+                def _():
+                    arrived(5, first), arrived(5, second)
+
             def rows_of(j):
                 return jnp.concatenate(
                     [recv[q][s * CAP + within(pos_s[k, 0, ahead * GROUP + dy * 2 * REG + j], CAP)]
@@ -381,7 +397,7 @@
         lax.fori_loop(0, NARROW // 2, regions, 0)
 
         raw = acc[0:size].T
-        gap = jnp.concatenate([meta_r[k, 0:GROUP, 0:2 * SAMP].astype(F32) for k in chunk], axis=1)
+        gap = jnp.concatenate([meta_r[k, :, 0:2 * SAMP].astype(F32) for k in chunk], axis=1)
         density = raw[0:GROUP]
         density = jnp.maximum(density, 0.0) + jnp.log1p(jnp.exp(-jnp.abs(density)))
         optical = density * gap
@@ -394,14 +410,14 @@
         result = result[:, 0:128] + result[:, 128:256]
         for s, k in enumerate(chunk):
             target = ret_s if k else ret_r
-            target[k, 0:2, :] = result[2 * s:2 * s + 2]
+            target[k] = result[2 * s:2 * s + 2]
             if k:
                 returns[k] = remote(ret_s.at[k], ret_r.at[k], ret_ss.at[k], ret_rs.at[k], wide_at(k, -1))
                 returns[k].start()
 
     for k in range(1, WIDE):
         returns[k].wait_recv()
-    back = jnp.concatenate([ret_r[k, 0:2, :] for k in range(WIDE)], axis=0)
+    back = jnp.concatenate([ret_r[k] for k in range(WIDE)], axis=0)
     found = tn(halves(back), where_row[...])
     for c in range(4):
         fin_s[c:c + 1, :] = jnp.sum(found[c * GROUP:(c + 1) * GROUP] * keep[...], axis=0, keepdims=True)
@@ -412,13 +428,14 @@
     for s in range(1, NARROW):
         flags[s].wait_recv()
         flag = jnp.maximum(flag, flag_r[s])
-    over_out[...] = jnp.broadcast_to(flag[0:1, FLAG:FLAG + 1], (1, 128))
+    over_out[...] = jnp.broadcast_to(flag[:, FLAG:FLAG + 1], (1, 128))
     for s in range(1, NARROW):
         for copy in weights[s]:
             copy.wait_send()
         flags[s].wait_send()
     for k in range(1, WIDE):
         metas[k].wait_send()
+        places[k].wait_send()
         data_copy(k, 0, CAP).wait_send()
         returns[k].wait_send()
     for k in range(1, WIDE):
@@ -447,16 +464,16 @@
     scratch += [vmem((len(chunk) * CAP, SAMP, FEAT), BF16) for chunk in CHUNKS]
     scratch += [
         vmem((regions, FEAT, HID), BF16), vmem((regions, 2, HID, HID), BF16), vmem((NARROW, REG, 4, HID), BF16),
-        vmem((regions * HID, 128), BF16), vmem((WIDE, META, 128), BF16), vmem((WIDE, META, 128), BF16),
-        vmem((WIDE, 8, 128), I32), smem((WIDE, 8, 128), I32), vmem((WIDE, 128), I32), smem((WIDE, 128), I32),
+        vmem((regions * HID, 128), BF16), vmem((WIDE, GROUP, 128), BF16), vmem((WIDE, GROUP, 128), BF16),
+        vmem((WIDE, 1, 128), I32), vmem((WIDE, 1, 128), I32), smem((WIDE, 1, 128), I32), vmem((WIDE, 128), I32), smem((WIDE, 128), I32),
         vmem((MOST, 128), F32), vmem((MOST, MOST), BF16), vmem((16, MOST), BF16), vmem((4 * WIDE, ROWS), BF16),
-        vmem((GROUP, ROWS), F32), vmem((WIDE, 8, 128), F32), vmem((WIDE, 8, 128), F32),
-        vmem((8, ROWS), F32), vmem((WIDE, 8, ROWS), F32), vmem((8, 128), F32), vmem((NARROW, 8, 128), F32),
-        dma((9,)), dma((5, NARROW)), dma((5, NARROW)), dma((WIDE,)), dma((WIDE,)), dma((WIDE,)),
+        vmem((GROUP, ROWS), F32), vmem((WIDE, 2, 128), F32), vmem((WIDE, 2, 128), F32),
+        vmem((4, ROWS), F32), vmem((WIDE, 4, ROWS), F32), vmem((1, 128), I32), vmem((NARROW, 1, 128), I32),
+        dma((9,)), dma((5, NARROW)), dma((5, NARROW)), dma((WIDE,)), dma((WIDE,)), dma((WIDE,)), dma((WIDE,)), dma((WIDE,)),
         dma((WIDE,)), dma((WIDE,)), dma((WIDE,)), dma((WIDE,)), dma((WIDE,)), dma((NARROW,)), dma((NARROW,))]
     return pl.pallas_call(
         render_kernel,
-        out_shape=(jax.ShapeDtypeStruct((3, ROWS), F32), jax.ShapeDtypeStruct((1, 128), F32)),
+        out_shape=(jax.ShapeDtypeStruct((3, ROWS), F32), jax.ShapeDtypeStruct((1, 128), I32)),
         in_specs=[any_place, whole, whole, whole, any_place, any_place, any_place],
         out_specs=(whole, whole),
         scratch_shapes=scratch,

time: 122 us -> 118 us (0.967)
  Pallas kernels: 120 us -> 116 us
    pallas_call x1, Pallas kernels: 120 us -> 116 us  [render(): pl.pallas_call(render_kernel, out_shape=(jax.ShapeDtypeStruct((3, ROWS),...]
where the time goes in v3:
time: 118 us
  Pallas kernels  116 us (98%)
    pallas_call x1, Pallas kernels, render(): pl.pallas_call(render_kernel, out_shape=(jax.ShapeDtypeStruct((3, ROWS),...  116 us

profile of v3, /device:TPU:0, one launch (start us, length us, event | category | flops | bytes accessed | tf_op | source)
XLA Modules:
  0.0 117.6 jit_solution(16018376036665714469)
XLA Ops:
  0.0 0.0 copy-start.2
  0.0 0.0 copy-start.10
  0.0 116.0 %render.1 = (f32[3,512]{1,0:T(4,128)S(1)}, s32[1,128]{1,0:T(1,128)}) custom-call(bf16[512,48,128]{2,1,0:T(8,128)(2,1)} %bitcast.169, bf16[48,512]{1,0:T(8,128)(2,1)} %bitcast.182, s32[1,512]{1,0:T(1,128)} %bitcast.183, s32[1,512]{1,0:T(1,128)} %bitcast.189, bf16[4,128,256]{2,1,0:T(8,128)(2,1)} %w_in.1, bf16[4,2,256,256]{3,2,1,0:T(8,128)(2,1)} %w_mid.1, ...), custom_call_target="tpu_custom_call" | custom-call | tf_op jit(solution)/shard_map/render/pallas_call | solution.py:474
  116.7 0.0 copy-done.2
  116.7 0.0 copy-done.10
  116.7 0.2 conditional.1
  117.0 0.6 copy.359
Async XLA Ops:
  0.0 116.7 %copy-start.2 = (bf16[1,512,48]{1,2,0:T(8,128)(2,1)S(1)}, bf16[1,512,48]{1,2,0:T(8,128)(2,1)}, u32[]{:S(2)}) copy-start(bf16[1,512,48]{1,2,0:T(8,128)(2,1)} %param.14) | copy-start | bytes 147460
  0.0 116.7 %copy-start.10 = (s32[1,512,1]{1,2,0:T(1,128)S(1)}, s32[1,512,1]{1,2,0:T(1,128)}, u32[]{:S(2)}) copy-start(s32[1,512,1]{1,2,0:T(1,128)} %param.15) | copy-start | bytes 6148

commit v4 on v3

--- a/solution.py
+++ b/solution.py
@@ -10,7 +10,7 @@
 ROWS, SAMP, FEAT, HID = 512, 48, 128, 256
 WIDE, NARROW, REG, GROUP = 16, 8, 4, 32
 CAP = 40
-PIECE = 8
+PIECE = 4
 FLAG = 127
 
 SEND_ORDER = ((6, 14, 9, 11, 1, 3, 4, 12), (2, 8, 10))

time: 118 us -> 115 us (0.975)
  Pallas kernels: 116 us -> 114 us
    pallas_call x1, Pallas kernels: 116 us -> 114 us  [render(): pl.pallas_call(render_kernel, out_shape=(jax.ShapeDtypeStruct((3, ROWS),...]
where the time goes in v4:
time: 115 us
  Pallas kernels  114 us (99%)
    pallas_call x1, Pallas kernels, render(): pl.pallas_call(render_kernel, out_shape=(jax.ShapeDtypeStruct((3, ROWS),...  114 us

profile of v4, /device:TPU:0, one launch (start us, length us, event | category | flops | bytes accessed | tf_op | source)
XLA Modules:
  0.0 115.2 jit_solution(1008398749190312183)
XLA Ops:
  0.0 0.0 copy-start.2
  0.0 0.0 copy-start.10
  0.0 113.6 %render.1 = (f32[3,512]{1,0:T(4,128)S(1)}, s32[1,128]{1,0:T(1,128)}) custom-call(bf16[512,48,128]{2,1,0:T(8,128)(2,1)} %bitcast.169, bf16[48,512]{1,0:T(8,128)(2,1)} %bitcast.182, s32[1,512]{1,0:T(1,128)} %bitcast.183, s32[1,512]{1,0:T(1,128)} %bitcast.189, bf16[4,128,256]{2,1,0:T(8,128)(2,1)} %w_in.1, bf16[4,2,256,256]{3,2,1,0:T(8,128)(2,1)} %w_mid.1, ...), custom_call_target="tpu_custom_call" | custom-call | tf_op jit(solution)/shard_map/render/pallas_call | solution.py:474
  114.3 0.0 copy-done.2
  114.3 0.0 copy-done.10
  114.3 0.2 conditional.1
  114.5 0.6 copy.359
Async XLA Ops:
  0.0 114.3 %copy-start.2 = (bf16[1,512,48]{1,2,0:T(8,128)(2,1)S(1)}, bf16[1,512,48]{1,2,0:T(8,128)(2,1)}, u32[]{:S(2)}) copy-start(bf16[1,512,48]{1,2,0:T(8,128)(2,1)} %param.14) | copy-start | bytes 147460
  0.0 114.3 %copy-start.10 = (s32[1,512,1]{1,2,0:T(1,128)S(1)}, s32[1,512,1]{1,2,0:T(1,128)}, u32[]{:S(2)}) copy-start(s32[1,512,1]{1,2,0:T(1,128)} %param.15) | copy-start | bytes 6148

commit v5 on v4

--- a/solution.py
+++ b/solution.py
@@ -254,6 +254,9 @@
                     (1, last), (1, first), (1, second)):
         start(s, part)
 
+    pack(1, SEND_ORDER[0])
+    pack(2, SEND_ORDER[0])
+
     nb = jnp.bitwise_and(jnp.right_shift(rid, 2), 7)
     t = jnp.bitwise_and(jnp.right_shift(nb, 1) - y, 3) * 2 + jnp.bitwise_and(nb + core, 1)
     r = t * REG + jnp.bitwise_and(rid, 3)
@@ -287,7 +290,7 @@
         lax.fori_loop(begin, CAP // PIECE, step, 0)
 
     for i, order in enumerate(SEND_ORDER):
-        pack_all(order, 1 if i == 0 else 0)
+        pack_all(order, 3 if i == 0 else 0)
 
     def pack_own(piece, carry):
         q, s = place[0]

time: 115 us -> 115 us (level)
  no operation moved by 1% of the time
where the time goes in v5:
time: 115 us
  Pallas kernels  113 us (98%)
    pallas_call x1, Pallas kernels, render(): pl.pallas_call(render_kernel, out_shape=(jax.ShapeDtypeStruct((3, ROWS),...  113 us

profile of v5, /device:TPU:0, one launch (start us, length us, event | category | flops | bytes accessed | tf_op | source)
XLA Modules:
  0.0 115.0 jit_solution(6971526026076499819)
XLA Ops:
  0.0 0.0 copy-start.2
  0.0 0.0 copy-start.10
  0.0 113.4 %render.1 = (f32[3,512]{1,0:T(4,128)S(1)}, s32[1,128]{1,0:T(1,128)}) custom-call(bf16[512,48,128]{2,1,0:T(8,128)(2,1)} %bitcast.169, bf16[48,512]{1,0:T(8,128)(2,1)} %bitcast.182, s32[1,512]{1,0:T(1,128)} %bitcast.183, s32[1,512]{1,0:T(1,128)} %bitcast.189, bf16[4,128,256]{2,1,0:T(8,128)(2,1)} %w_in.1, bf16[4,2,256,256]{3,2,1,0:T(8,128)(2,1)} %w_mid.1, ...), custom_call_target="tpu_custom_call" | custom-call | tf_op jit(solution)/shard_map/render/pallas_call | solution.py:477
  114.1 0.0 copy-done.2
  114.1 0.0 copy-done.10
  114.1 0.2 conditional.1
  114.4 0.6 copy.359
Async XLA Ops:
  0.0 114.1 %copy-start.2 = (bf16[1,512,48]{1,2,0:T(8,128)(2,1)S(1)}, bf16[1,512,48]{1,2,0:T(8,128)(2,1)}, u32[]{:S(2)}) copy-start(bf16[1,512,48]{1,2,0:T(8,128)(2,1)} %param.14) | copy-start | bytes 147460
  0.0 114.1 %copy-start.10 = (s32[1,512,1]{1,2,0:T(1,128)S(1)}, s32[1,512,1]{1,2,0:T(1,128)}, u32[]{:S(2)}) copy-start(s32[1,512,1]{1,2,0:T(1,128)} %param.15) | copy-start | bytes 6148
